TPU v7x, 32 devices: a whole 2x2x4 slice. The times are simulated.
32 devices in a mesh: grp: 4 (over x, core), ex: 8 (over z, y).
Axes of the slice: x: 2, y: 2, z: 4, core: 2. Of those that a mesh axis runs over, the one named last changes fastest.
Arguments:
- item_ids: int32 [64, 256], P(('grp', 'ex')), may hold values from 0 to 32767, as said below
- lengths: int32 [64], P(('grp', 'ex')), may hold values from 32 to 256
- expert_ids: int32 [16384, 2], P(('grp', 'ex')), may hold values from 0 to 31, all different within a row; in each aligned block of 512 rows (0 to 511, 512 to 1023, ...) at most 48 rows name the same one
- gate_weights: float32 [16384, 2], P(('grp', 'ex')), may hold values from 0.1 to 1
- table: bfloat16 [32768, 512], P('ex'), may hold values from -6 to 6
- norm_gain: float32 [512], replicated, may hold values from 0.1 to 1.9
- w_gate: bfloat16 [32, 512, 1024], P('ex'), may hold values from -0.25 to 0.25
- w_up: bfloat16 [32, 512, 1024], P('ex'), may hold values from -0.25 to 0.25
- w_down: bfloat16 [32, 512, 1024], P('ex'), may hold values from -0.1875 to 0.1875
- d_out: bfloat16 [16384, 512], P(('grp', 'ex')), may hold values from -0.59765625 to 0.59765625
Outputs:
- layer_out: bfloat16 [16384, 512], P(('grp', 'ex'))
- grad_gate: float32 [32, 512, 1024], P('ex', None, 'grp')
- grad_up: float32 [32, 512, 1024], P('ex', None, 'grp')
- grad_down: float32 [32, 512, 1024], P('ex', None, 'grp')
Inputs may be any that keep to these rules, and one draw needn't show every extreme that they name: `item_ids`: split the ids into blocks of 4096 consecutive values. Among the 512 positions of each aligned run of 2 sequences, at most 128 name ids of one such block, and in every such run some block is named exactly 128 times. `expert_ids`: each token names 2 different experts. Within each aligned block of 512 tokens no expert is named more than 48 times, and in some block some expert is named exactly 48 times.
All inputs are finite; a program needn't handle non-finite values.
Results may differ from a plain program's by a relative error of at most 0.012.
Values may be sent and summed in bfloat16 or wider, within the bound.
A program may use at most 128 MiB of HBM per device.

v0:
```python
import jax
import jax.numpy as jnp
from jax import lax
from jax.sharding import PartitionSpec as P

TOP = 2
CAP = 48


EPSILON = 1e-06


def silu_parts(pre):
    sigmoid = jax.nn.sigmoid(pre)
    return (sigmoid, pre * sigmoid)


def on_device(
    item_ids, lengths, expert_ids, gate_weights, table, norm_gain, w_gate, w_up, w_down, d_out
):
    ex_count = lax.axis_size("ex")
    seqs_here, seq_len = item_ids.shape
    tok_here = seqs_here * seq_len
    rows_here, width = table.shape
    exp_here = w_gate.shape[0]
    experts_all = exp_here * ex_count
    every_id = lax.all_gather(item_ids, "ex", axis=0, tiled=True).reshape(-1)
    my_shard = lax.axis_index("ex")
    first_row = my_shard * rows_here
    row_cap = tok_here // 4
    mine = (every_id // rows_here == my_shard).astype(jnp.int32).reshape(ex_count, tok_here)
    order = jnp.cumsum(mine, axis=1) - mine
    requester = lax.broadcasted_iota(jnp.int32, (ex_count, tok_here), 0)
    dump = ex_count * row_cap
    slot = jnp.where(mine == 1, requester * row_cap + order, dump).reshape(-1)
    local_rows = jnp.clip(every_id - first_row, 0, rows_here - 1)
    index_buffer = jnp.zeros((dump + 1,), jnp.int32).at[slot].set(local_rows)[:dump]
    packed = jnp.take(table, index_buffer, axis=0).reshape(ex_count, row_cap, width)
    arrived = lax.all_to_all(packed, "ex", split_axis=0, concat_axis=0, tiled=True)
    own_ids = item_ids.reshape(-1)
    own_shard = own_ids // rows_here
    shard_iota = lax.broadcasted_iota(jnp.int32, (1, ex_count), 1)
    shard_hot = (own_shard[:, None] == shard_iota).astype(jnp.int32)
    own_rank = jnp.sum((jnp.cumsum(shard_hot, axis=0) - shard_hot) * shard_hot, axis=1)
    found = jnp.take(
        arrived.reshape(ex_count * row_cap, width), own_shard * row_cap + own_rank, axis=0
    ).astype(jnp.float32)
    position = lax.broadcasted_iota(jnp.int32, (seqs_here, seq_len), 1)
    valid = (position < lengths[:, None]).reshape(tok_here)
    embedded = jnp.where(valid[:, None], found, 0.0)
    mean_square = jnp.mean(embedded * embedded, axis=1, keepdims=True)
    normed = (embedded * lax.rsqrt(mean_square + EPSILON) * norm_gain[None, :]).astype(jnp.bfloat16)
    cotangent = (gate_weights[:, :, None] * d_out[:, None, :].astype(jnp.float32)).astype(
        jnp.bfloat16
    )
    expert_iota = lax.broadcasted_iota(jnp.int32, (1, experts_all), 1)
    onehot = (expert_ids.reshape(-1)[:, None] == expert_iota).astype(jnp.int32)
    earlier = jnp.cumsum(onehot, axis=0) - onehot
    rank = jnp.sum(earlier * onehot, axis=1).reshape(tok_here, TOP)
    slots = expert_ids * CAP + rank
    outbound = jnp.zeros((experts_all * CAP, width), jnp.bfloat16)
    send_rows = outbound.at[slots].set(jnp.broadcast_to(normed[:, None, :], (tok_here, TOP, width)))
    send_cot = outbound.at[slots].set(cotangent)
    inbound_rows, inbound_cot = (
        lax.all_to_all(
            send_rows.reshape(ex_count, exp_here * CAP, width),
            "ex",
            split_axis=0,
            concat_axis=0,
            tiled=True,
        ),
        lax.all_to_all(
            send_cot.reshape(ex_count, exp_here * CAP, width),
            "ex",
            split_axis=0,
            concat_axis=0,
            tiled=True,
        ),
    )
    inbound_rows = inbound_rows.reshape(ex_count, exp_here, CAP, width)
    inbound_cot = inbound_cot.reshape(ex_count, exp_here, CAP, width)
    gate_pre = jnp.einsum(
        "sjcd,jdf->sjcf", inbound_rows, w_gate, preferred_element_type=jnp.float32
    )
    up_pre = jnp.einsum("sjcd,jdf->sjcf", inbound_rows, w_up, preferred_element_type=jnp.float32)
    sigmoid, silu_gate = silu_parts(gate_pre)
    active = (silu_gate * up_pre).astype(jnp.bfloat16)
    expert_out = jnp.einsum(
        "sjcf,jdf->sjcd", active, w_down, preferred_element_type=jnp.float32
    ).astype(jnp.bfloat16)
    returned = lax.all_to_all(
        expert_out.reshape(ex_count, exp_here * CAP, width),
        "ex",
        split_axis=0,
        concat_axis=0,
        tiled=True,
    )
    gathered_out = jnp.take(returned.reshape(experts_all * CAP, width), slots, axis=0)
    mixed = embedded + jnp.sum(gate_weights[:, :, None] * gathered_out.astype(jnp.float32), axis=1)
    output = mixed.astype(jnp.bfloat16)
    part_down = jnp.einsum(
        "sjcd,sjcf->jdf", inbound_cot, active, preferred_element_type=jnp.float32
    )
    d_active = jnp.einsum("sjcd,jdf->sjcf", inbound_cot, w_down, preferred_element_type=jnp.float32)
    d_gate = (d_active * up_pre * sigmoid * (1.0 + gate_pre * (1.0 - sigmoid))).astype(jnp.bfloat16)
    d_up = (d_active * silu_gate).astype(jnp.bfloat16)
    part_gate = jnp.einsum(
        "sjcd,sjcf->jdf", inbound_rows, d_gate, preferred_element_type=jnp.float32
    )
    part_up = jnp.einsum("sjcd,sjcf->jdf", inbound_rows, d_up, preferred_element_type=jnp.float32)
    part_gate, part_up = (part_gate, part_up)
    grad_gate, grad_up, grad_down = (
        lax.psum_scatter(
            part_gate.astype(jnp.bfloat16), "grp", scatter_dimension=2, tiled=True
        ).astype(jnp.float32),
        lax.psum_scatter(
            part_up.astype(jnp.bfloat16), "grp", scatter_dimension=2, tiled=True
        ).astype(jnp.float32),
        lax.psum_scatter(
            part_down.astype(jnp.bfloat16), "grp", scatter_dimension=2, tiled=True
        ).astype(jnp.float32),
    )
    return (output, grad_gate, grad_up, grad_down)


def solution(mesh):
    placed = (
        P(("grp", "ex"), None),
        P(("grp", "ex")),
        P(("grp", "ex"), None),
        P(("grp", "ex"), None),
        P("ex", None),
        P(),
        P("ex", None, None),
        P("ex", None, None),
        P("ex", None, None),
        P(("grp", "ex"), None),
    )
    return jax.shard_map(
        on_device,
        mesh=mesh,
        in_specs=placed,
        out_specs=(
            P(("grp", "ex"), None),
            P("ex", None, "grp"),
            P("ex", None, "grp"),
            P("ex", None, "grp"),
        ),
        check_vma=False,
    )
```

profile of v0, /device:TPU:0, one launch (start us, length us, event | category | flops | bytes accessed | tf_op | source)
XLA Modules:
  0.0 338.0 jit_solution(1297884717571269889)
XLA Ops:
  7.2 27.9 %all-gather = s32[8,2,256]{2,1,0:T(2,128)S(1)} all-gather(s32[1,2,256]{2,1,0:T(2,128)} %bitcast.143), channel_id=1, replica_groups=mesh['grp'=4,'ex'=8] {'ex'}, dimensions={0}, use_global_device_ids=true | all-gather | bytes 18432 | tf_op jit(solution)/shard_map/all_gather | solution.py:27
  35.2 1.1 reduce-window.24
  36.3 0.2 slice_reduce_fusion
  36.6 0.1 broadcast_add_fusion.1
  36.7 0.1 broadcast_bitcast_fusion
  36.8 0.1 compare_select_fusion
  36.9 15.5 %scatter_custom_fusion = s32[1025]{0:T(1024)S(1)} fusion(s32[4096]{0:T(1024)S(1)} %bitcast.151, s32[4096]{0:T(1024)S(1)} %bitcast.150, s32[]{:T(128)} %constant.63.clone.1), kind=kCustom, calls=%fused_computation.100 | custom fusion | bytes 4104 | tf_op jit(solution)/shard_map/scatter | solution.py:37
  52.5 6.7 %gather_fusion = bf16[1024,512]{1,0:T(8,128)(2,1)S(1)} fusion(bf16[4096,512]{1,0:T(8,128)(2,1)} %param.14, s32[1024]{0:T(1024)S(1)} %fusion.44), kind=kCustom, calls=%fused_computation | custom fusion | bytes 2101248 | tf_op jit(solution)/shard_map/jit(_take)/gather | solution.py:38
  59.3 1.2 broadcast_select_fusion.1
  60.4 3.9 %all-to-all-start = ((bf16[8,128,512]{2,1,0:T(8,128)(2,1)}), bf16[8,128,512]{2,1,0:T(8,128)(2,1)S(1)}, u32[]{:S(2)}, u32[]{:S(2)}) async-start(bf16[8,128,512]{2,1,0:T(8,128)(2,1)} %broadcast_select_fusion.1), calls=%async_computation | async-start | bytes 2097152 | tf_op jit(solution)/shard_map/all_to_all | solution.py:39
  64.4 0.1 copy.64
  64.5 0.2 eq.93
  64.7 0.2 eq.89
  64.9 1.1 reduce-window.20
  66.0 0.2 slice_reduce_fusion.1
  66.3 0.1 iota_compare_fusion.4
  66.4 9.0 %reduce-window.26 = s32[32,8,128]{2,1,0:T(8,128)S(1)} reduce-window(s32[32,8,128]{2,1,0:T(8,128)S(1)} %fusion.36, s32[]{:T(128)} %constant.63.clone.1), window={size=1x1x128 pad=0_0x0_0x127_0}, to_apply=%region_6.7 | reduce-window | flops 4161536 | bytes 262148 | tf_op jit(solution)/shard_map/reduce-window.4
  75.4 0.1 slice.40
  75.5 0.1 copy.66
  75.7 0.1 copy.67
  75.8 0.1 broadcast_add_fusion
  75.9 0.2 reshape.440
  76.1 0.1 copy.68
  76.3 0.1 copy.70
  76.4 0.2 reshape.481
  76.6 0.1 fusion.40
  76.8 9.6 %all-to-all-done = bf16[8,128,512]{2,1,0:T(8,128)(2,1)S(1)} async-done(((bf16[8,128,512]{2,1,0:T(8,128)(2,1)}), bf16[8,128,512]{2,1,0:T(8,128)(2,1)S(1)}, u32[]{:S(2)}, u32[]{:S(2)}) %all-to-all-start) | async-done | bytes 1048608 | tf_op jit(solution)/shard_map/all_to_all | solution.py:39
  86.3 2.0 gather_fusion.1
  88.3 0.4 multiply_reduce_fusion.1
  88.7 0.3 multiply_convert_fusion.1
  89.0 0.5 broadcast_in_dim.84
  89.6 0.4 reshape.483
  90.0 6.4 %scatter_custom_fusion.1 = bf16[1536,512]{1,0:T(8,128)(2,1)} fusion(s32[1024]{0:T(1024)S(1)} %reshape.481, bf16[1024,512]{1,0:T(8,128)(2,1)S(1)} %reshape.483, bf16[]{:T(256)} %constant.104.clone.1), kind=kCustom, calls=%fused_computation.50 | custom fusion | bytes 1572866 | tf_op jit(solution)/shard_map/scatter | solution.py:62
  96.4 3.8 %all-to-all-start.1 = ((bf16[8,192,512]{2,1,0:T(8,128)(2,1)}), bf16[8,192,512]{2,1,0:T(8,128)(2,1)S(1)}, u32[]{:S(2)}, u32[]{:S(2)}) async-start(bf16[8,192,512]{2,1,0:T(8,128)(2,1)} %bitcast.137), calls=%async_computation.1 | async-start | bytes 3145728 | tf_op jit(solution)/shard_map/all_to_all | solution.py:65
  100.2 0.1 copy.63
  100.3 0.1 convert_element_type.102
  100.5 1.0 multiply_convert_fusion
  101.5 1.2 reshape.491
  102.7 6.9 %scatter_custom_fusion.2 = bf16[1536,512]{1,0:T(8,128)(2,1)} fusion(s32[1024]{0:T(1024)S(1)} %reshape.481, bf16[1024,512]{1,0:T(8,128)(2,1)} %reshape.491, bf16[]{:T(256)} %constant.104.clone.1), kind=kCustom, calls=%fused_computation.48 | custom fusion | bytes 1573376 | tf_op jit(solution)/shard_map/scatter | solution.py:63
  109.6 26.2 %all-to-all-done.1 = bf16[8,192,512]{2,1,0:T(8,128)(2,1)S(1)} async-done(((bf16[8,192,512]{2,1,0:T(8,128)(2,1)}), bf16[8,192,512]{2,1,0:T(8,128)(2,1)S(1)}, u32[]{:S(2)}, u32[]{:S(2)}) %all-to-all-start.1) | async-done | bytes 1572896 | tf_op jit(solution)/shard_map/all_to_all | solution.py:65
  135.7 4.3 %all-to-all-start.3 = ((bf16[8,192,512]{2,1,0:T(8,128)(2,1)}), bf16[8,192,512]{2,1,0:T(8,128)(2,1)}, u32[]{:S(2)}, u32[]{:S(2)}) async-start(bf16[8,192,512]{2,1,0:T(8,128)(2,1)} %bitcast.136), calls=%async_computation.3 | async-start | bytes 3145728 | tf_op jit(solution)/shard_map/all_to_all | solution.py:72
  140.0 0.0 reduce-scatter.6.cloned.1.call-start
  140.1 6.8 %fusion.11 = f32[4,8,48,1024]{3,2,1,0:T(8,128)} fusion(bf16[4,512,1024]{2,1,0:T(8,128)(2,1)} %param.16, bf16[8,4,48,512]{3,2,1,0:T(8,128)(2,1)S(1)} %bitcast.132), kind=kOutput, calls=%fused_computation.26 | convolution fusion | flops 1610612736 | bytes 12058624 | tf_op jit(solution)/shard_map/sjcd,jdf->sjcf/dot_general | solution.py:82
  146.9 4.5 %fusion.9 = f32[4,8,48,1024]{3,2,1,0:T(8,128)} fusion(bf16[4,512,1024]{2,1,0:T(8,128)(2,1)S(1)} %copy-done, bf16[8,4,48,512]{3,2,1,0:T(8,128)(2,1)S(1)} %bitcast.133), kind=kOutput, calls=%fused_computation.24 | convolution fusion | flops 1610612736 | bytes 12058624 | tf_op jit(solution)/shard_map/sjcd,jdf->sjcf/dot_general | solution.py:85
  151.3 25.0 %all-to-all-done.3 = bf16[8,192,512]{2,1,0:T(8,128)(2,1)} async-done(((bf16[8,192,512]{2,1,0:T(8,128)(2,1)}), bf16[8,192,512]{2,1,0:T(8,128)(2,1)}, u32[]{:S(2)}, u32[]{:S(2)}) %all-to-all-start.3) | async-done | bytes 1572896 | tf_op jit(solution)/shard_map/all_to_all | solution.py:72
  176.4 10.0 %fusion.3 = (bf16[8,4,48,1024]{3,2,0,1:T(8,128)(2,1)S(1)}, bf16[8,4,48,1024]{3,2,0,1:T(8,128)(2,1)}, bf16[8,4,48,1024]{3,2,0,1:T(8,128)(2,1)}) fusion(f32[4,8,48,1024]{3,2,1,0:T(8,128)} %fusion.11, f32[4,8,48,1024]{3,2,1,0:T(8,128)} %fusion.9, bf16[4,512,1024]{2,1,0:T(8,128)(2,1)} %param.18, bf16[8,4,48,512]{3,2,1,0:T(8,128)(2,1)} %bitcast.26), kind=kOutput, calls=%fused_computation.14 | convolution fusion | flops 1634205696 | bytes 27787264 | tf_op jit(solution)/shard_map/sjcd,jdf->sjcf/dot_general | solution.py:104
  186.4 4.4 %bitcast_convert_fusion.1 = bf16[4,512,1024]{2,1,0:T(8,128)(2,1)} fusion(bf16[8,4,48,512]{3,2,1,0:T(8,128)(2,1)S(1)} %bitcast.134, bf16[8,4,48,1024]{3,2,0,1:T(8,128)(2,1)S(1)} %get-tuple-element.6), kind=kOutput, calls=%fused_computation.7 | convolution fusion | flops 1612709888 | bytes 8912896 | tf_op jit(solution)/shard_map/sjcd,sjcf->jdf/dot_general | solution.py:110
  190.8 0.3 reduce-scatter.4.cloned.1.call-start
  191.1 6.2 %bitcast_convert_fusion.2 = bf16[4,512,1024]{2,1,0:T(8,128)(2,1)} fusion(bf16[8,4,48,512]{3,2,1,0:T(8,128)(2,1)S(1)} %bitcast.135, bf16[8,4,48,1024]{3,2,0,1:T(8,128)(2,1)} %get-tuple-element.7), kind=kOutput, calls=%fused_computation.8 | convolution fusion | flops 1612709888 | bytes 8912896 | tf_op jit(solution)/shard_map/sjcd,sjcf->jdf/dot_general | solution.py:107
  197.3 7.6 %bitcast_convert_fusion = bf16[4,512,1024]{2,1,0:T(8,128)(2,1)} fusion(bf16[8,4,48,512]{3,2,1,0:T(8,128)(2,1)} %bitcast.26, bf16[8,4,48,1024]{3,2,0,1:T(8,128)(2,1)} %get-tuple-element.8), kind=kOutput, calls=%fused_computation.6 | convolution fusion | flops 1612709888 | bytes 8912896 | tf_op jit(solution)/shard_map/sjcd,sjcf->jdf/dot_general | solution.py:101
  205.0 5.0 %fusion.24 = bf16[8,4,48,512]{3,2,0,1:T(8,128)(2,1)S(1)} fusion(bf16[8,4,48,1024]{3,2,0,1:T(8,128)(2,1)} %get-tuple-element.8, bf16[4,512,1024]{2,1,0:T(8,128)(2,1)} %param.18), kind=kOutput, calls=%fused_computation.40 | convolution fusion | flops 1611399168 | bytes 8912896 | tf_op jit(solution)/shard_map/sjcf,jdf->sjcd/dot_general | solution.py:88
  209.9 1.3 copy.73
  211.2 3.6 %all-to-all-start.2 = ((bf16[8,192,512]{2,1,0:T(8,128)(2,1)}), bf16[8,192,512]{2,1,0:T(8,128)(2,1)S(1)}, u32[]{:S(2)}, u32[]{:S(2)}) async-start(bf16[8,192,512]{2,1,0:T(8,128)(2,1)} %bitcast.138), calls=%async_computation.2 | async-start | bytes 3145728 | tf_op jit(solution)/shard_map/all_to_all | solution.py:91
  214.8 0.2 copy.69
  215.0 36.4 %all-to-all-done.2 = bf16[8,192,512]{2,1,0:T(8,128)(2,1)S(1)} async-done(((bf16[8,192,512]{2,1,0:T(8,128)(2,1)}), bf16[8,192,512]{2,1,0:T(8,128)(2,1)S(1)}, u32[]{:S(2)}, u32[]{:S(2)}) %all-to-all-start.2) | async-done | bytes 1572896 | tf_op jit(solution)/shard_map/all_to_all | solution.py:91
  251.4 4.0 %gather_fusion.2 = bf16[1024,512]{1,0:T(8,128)(2,1)S(1)} fusion(bf16[1536,512]{1,0:T(8,128)(2,1)S(1)} %bitcast.130, s32[1024]{0:T(1024)S(1)} %broadcast_clamp_fusion), kind=kCustom, calls=%fused_computation.2 | custom fusion | bytes 2101248 | tf_op jit(solution)/shard_map/jit(_take)/gather | solution.py:98
  255.4 0.4 reshape.464
  255.8 4.4 %multiply_reduce_fusion = f32[512,512]{1,0:T(8,128)S(1)} fusion(bf16[512,2,512]{2,1,0:T(2,128)(2,1)S(1)} %reshape.464, pred[512,2]{1,0:T(8,128)(4,1)S(1)} %copy.69, f32[512,2]{1,0:T(8,128)S(1)} %copy.63), kind=kLoop, calls=%fused_computation.36 | loop fusion | flops 1835008 | bytes 2102272 | tf_op jit(solution)/shard_map/reduce_sum | solution.py:99
  260.2 1.0 add_convert_fusion
  261.2 2.7 convert_element_type.109
  264.0 17.7 %reduce-scatter.4.cloned.1.call-done = bf16[4,512,256]{2,1,0:T(8,128)(2,1)} async-done(((bf16[4,512,1024]{2,1,0:T(8,128)(2,1)}), bf16[4,512,256]{2,1,0:T(8,128)(2,1)}) %reduce-scatter.4.cloned.1.call-update) | async-done | bytes 1048592 | tf_op jit(solution)/shard_map/reduce_scatter | solution.py:113
  281.7 2.7 convert_element_type.106
  284.4 44.3 %reduce-scatter.8.cloned.1.call-done = bf16[4,512,256]{2,1,0:T(8,128)(2,1)} async-done(((bf16[4,512,1024]{2,1,0:T(8,128)(2,1)}), bf16[4,512,256]{2,1,0:T(8,128)(2,1)}) %reduce-scatter.8.cloned.1.call-update) | async-done | bytes 1048592 | tf_op jit(solution)/shard_map/reduce_scatter | solution.py:119
  328.8 2.7 convert_element_type.111
  (50 shorter events, 0.6 us)
Async XLA Ops:
  59.2 5.1 %copy-start.2 = (s32[2,256]{1,0:T(2,128)S(1)}, s32[2,256]{1,0:T(2,128)}, u32[]{:S(2)}) copy-start(s32[2,256]{1,0:T(2,128)} %param.10) | copy-start | bytes 6148
  59.2 5.1 %copy-start.3 = (s32[512,2]{0,1:T(2,128)S(1)}, s32[512,2]{0,1:T(2,128)}, u32[]{:S(2)}) copy-start(s32[512,2]{0,1:T(2,128)} %param.12) | copy-start | bytes 12292
  59.2 7.0 %copy-start.6 = (s32[2]{0:T(128)S(1)}, s32[2]{0:T(128)}, u32[]{:S(2)}) copy-start(s32[2]{0:T(128)} %param.11) | copy-start | bytes 28
  60.4 25.9 %all-to-all-start = ((bf16[8,128,512]{2,1,0:T(8,128)(2,1)}), bf16[8,128,512]{2,1,0:T(8,128)(2,1)S(1)}, u32[]{:S(2)}, u32[]{:S(2)}) async-start(bf16[8,128,512]{2,1,0:T(8,128)(2,1)} %broadcast_select_fusion.1), calls=%async_computation | async-start | bytes 2097152 | tf_op jit(solution)/shard_map/all_to_all | solution.py:39
  75.9 12.8 %copy-start.5 = (f32[512]{0:T(512)S(1)}, f32[512]{0:T(512)}, u32[]{:S(2)}) copy-start(f32[512]{0:T(512)} %param.15) | copy-start | bytes 6148
  89.6 10.6 %copy-start.4 = (f32[512,2]{0,1:T(2,128)S(1)}, f32[512,2]{0,1:T(2,128)}, u32[]{:S(2)}) copy-start(f32[512,2]{0,1:T(2,128)} %param.13) | copy-start | bytes 12292
  89.6 10.8 %copy-start.1 = (bf16[512,512]{1,0:T(8,128)(2,1)S(1)}, bf16[512,512]{1,0:T(8,128)(2,1)}, u32[]{:S(2)}) copy-start(bf16[512,512]{1,0:T(8,128)(2,1)} %param.19) | copy-start | bytes 1572868
  96.4 39.3 %all-to-all-start.1 = ((bf16[8,192,512]{2,1,0:T(8,128)(2,1)}), bf16[8,192,512]{2,1,0:T(8,128)(2,1)S(1)}, u32[]{:S(2)}, u32[]{:S(2)}) async-start(bf16[8,192,512]{2,1,0:T(8,128)(2,1)} %bitcast.137), calls=%async_computation.1 | async-start | bytes 3145728 | tf_op jit(solution)/shard_map/all_to_all | solution.py:65
  135.7 40.7 %all-to-all-start.3 = ((bf16[8,192,512]{2,1,0:T(8,128)(2,1)}), bf16[8,192,512]{2,1,0:T(8,128)(2,1)}, u32[]{:S(2)}, u32[]{:S(2)}) async-start(bf16[8,192,512]{2,1,0:T(8,128)(2,1)} %bitcast.136), calls=%async_computation.3 | async-start | bytes 3145728 | tf_op jit(solution)/shard_map/all_to_all | solution.py:72
  140.0 121.2 %reduce-scatter.6.cloned.1.call-start = ((), (), s32[]{:S(2)}) async-start(), calls=%async_computation.8 | async-start | bytes 5242880 | tf_op jit(solution)/shard_map/reduce_scatter | solution.py:116
  140.1 6.8 %copy-start = (bf16[4,512,1024]{2,1,0:T(8,128)(2,1)S(1)}, bf16[4,512,1024]{2,1,0:T(8,128)(2,1)}, u32[]{:S(2)}) copy-start(bf16[4,512,1024]{2,1,0:T(8,128)(2,1)} %param.17) | copy-start | bytes 12582916
  190.8 90.9 %reduce-scatter.4.cloned.1.call-start = ((), (), s32[]{:S(2)}) async-start(), calls=%async_computation.7 | async-start | bytes 5242880 | tf_op jit(solution)/shard_map/reduce_scatter | solution.py:113
  197.3 131.5 %reduce-scatter.8.cloned.1.call-start = ((), (), s32[]{:S(2)}) async-start(), calls=%async_computation.9 | async-start | bytes 5242880 | tf_op jit(solution)/shard_map/reduce_scatter | solution.py:119
  211.2 40.2 %all-to-all-start.2 = ((bf16[8,192,512]{2,1,0:T(8,128)(2,1)}), bf16[8,192,512]{2,1,0:T(8,128)(2,1)S(1)}, u32[]{:S(2)}, u32[]{:S(2)}) async-start(bf16[8,192,512]{2,1,0:T(8,128)(2,1)} %bitcast.138), calls=%async_computation.2 | async-start | bytes 3145728 | tf_op jit(solution)/shard_map/all_to_all | solution.py:91
Sparse Core Ops, SparseCore 0:
  190.9 43.5 reduce-scatter.5
  237.2 44.4 reduce-scatter.3
  284.2 44.4 reduce-scatter.7
where the time goes:
time: 339 us; the launch traced here: 338 us
  waiting for transfers between devices  159 us (47%)
  local copies, waits for them, and re-layouts  47.7 us (14%)
  matrix products  44.4 us (13%)
  other arithmetic  28.6 us (8%)
  blocking collectives  27.9 us (8%)
  starting transfers between devices  15.9 us (5%)
  between operations  14.2 us (4%)
    reduce_scatter x1, waiting for transfers between devices, on_device(): lax.psum_scatter(part_down.astype(jnp.bfloat16), 'grp', scatter_dimension...  44.3 us
    all_to_all x1, waiting for transfers between devices, on_device(): lax.all_to_all(expert_out.reshape(ex_count, exp_here * CAP, width), 'ex',...  36.4 us
    all_gather x1, blocking collectives, on_device(): every_id = lax.all_gather(item_ids, 'ex', axis=0, tiled=True).reshape(-1)  27.9 us
    all_to_all x1, waiting for transfers between devices, on_device(): lax.all_to_all(send_rows.reshape(ex_count, exp_here * CAP, width), 'ex',...  26.2 us
    all_to_all x1, waiting for transfers between devices, on_device(): lax.all_to_all(send_cot.reshape(ex_count, exp_here * CAP, width), 'ex', s...  25 us
    reduce_scatter x1, waiting for transfers between devices, on_device(): lax.psum_scatter(part_gate.astype(jnp.bfloat16), 'grp', scatter_dimension...  17.7 us
    scatter x1, local copies, waits for them, and re-layouts, on_device(): jnp.zeros((dump + 1,), jnp.int32).at[slot].set(local_rows)[:dump]  15.5 us
    another operation x8, other arithmetic  11.6 us
  transfers between devices with their start and end apart: 7, of which 6 were waited for; matrix products, arithmetic and copies ran while one was open for 20% of the time, Pallas kernels for 0%

commit v1 on v0

v1 whole, which is shorter than its diff:
```python
import functools

import jax
import jax.numpy as jnp
from jax import lax
from jax.experimental import pallas as pl
from jax.experimental.pallas import tpu as pltpu
from jax.sharding import PartitionSpec as P

TOP = 2
CAP = 48
EPSILON = 1e-06
VMEM_BYTES = 56 * 1024 * 1024
MESH = pl.DeviceIdType.MESH
BF = jnp.bfloat16
F32 = jnp.float32


def iota(shape, dim):
    return lax.broadcasted_iota(jnp.int32, shape, dim)


def dot(a, b, dims=((1,), (0,))):
    return lax.dot_general(a, b, (dims, ((), ())), preferred_element_type=F32)


def fetch_kernel(
    n, groups, seqs, experts, row_cap,
    ids_row, ids_col, lens, e_row, g_row, table, gain, d_out,
    rows_in, cot_all, embedded,
    all_ids, key, local, packed, arrived, chosen, send_cot, send_rows,
    ids_s, ids_r, row_s, row_r, cot_s, cot_r, nrm_s, nrm_r, grp_s, grp_f, grp_r, own,
):
    me = lax.axis_index("ex")
    grp = lax.axis_index("grp")
    chips = groups // 2
    chip, core = grp // 2, grp % 2
    mate = chip * 2 + 1 - core
    rows_here, width = table.shape
    tok = ids_row.shape[1]
    block = experts // n * CAP

    barrier = pltpu.get_barrier_semaphore()
    for d in range(1, n):
        pl.semaphore_signal(barrier, inc=1, device_id={"ex": lax.rem(me + d, n)}, device_id_type=MESH)
    for d in range(1, chips):
        peer = lax.rem(chip + d, chips) * 2 + core
        pl.semaphore_signal(barrier, inc=1, device_id={"grp": peer}, device_id_type=MESH)
    pl.semaphore_signal(barrier, inc=1, device_id={"grp": mate}, device_id_type=MESH)
    pl.semaphore_wait(barrier, n - 1 + chips)

    def to_ex(src, dst, send, recv, d):
        peer = lax.rem(me + d, n)
        return pltpu.make_async_remote_copy(
            src_ref=src(peer), dst_ref=dst, send_sem=send.at[d], recv_sem=recv.at[d],
            device_id={"ex": peer}, device_id_type=MESH,
        )

    def ids_copy(d):
        return to_ex(lambda p: all_ids.at[me], all_ids.at[me], ids_s, ids_r, d)

    def row_copy(d):
        return to_ex(lambda p: packed.at[p], arrived.at[me], row_s, row_r, d)

    def cot_copy(d):
        return to_ex(lambda p: send_cot.at[p], cot_all.at[grp, me], cot_s, cot_r, d)

    def nrm_copy(d):
        return to_ex(lambda p: send_rows.at[p], rows_in.at[me], nrm_s, nrm_r, d)

    all_ids[me] = ids_row[...]
    for d in range(1, n):
        ids_copy(d).start()

    before = (iota((tok, tok), 0) < iota((tok, tok), 1)).astype(BF)
    e0, e1 = e_row[0:1, :], e_row[1:2, :]
    e_iota = iota((experts, tok), 0)
    hot0, hot1 = e_iota == e0, e_iota == e1
    hot = jnp.where(hot0, 1.0, jnp.where(hot1, 1.0, 0.0)).astype(BF)
    earlier = dot(hot, before)
    slot0 = e0 * CAP + jnp.sum(jnp.where(hot0, earlier, 0.0), axis=0, keepdims=True).astype(jnp.int32)
    slot1 = e1 * CAP + jnp.sum(jnp.where(hot1, earlier, 0.0), axis=0, keepdims=True).astype(jnp.int32)
    g0, g1 = g_row[0:1, :], g_row[1:2, :]
    for p in range(n):
        s_iota = iota((block, tok), 0) + p * block
        m0, m1 = s_iota == slot0, s_iota == slot1
        weight = jnp.sum(jnp.where(m0, g0, jnp.where(m1, g1, 0.0)), axis=1, keepdims=True)
        chosen[p] = jnp.where(m0, 1.0, jnp.where(m1, 1.0, 0.0)).astype(BF)
        send_cot[p] = (weight * dot(chosen[p], d_out[...])).astype(BF)
    for d in range(1, n):
        cot_copy(d).start()
    own_cot = pltpu.make_async_copy(send_cot.at[me], cot_all.at[grp, me], own.at[0])
    own_cot.start()

    for d in range(1, n):
        ids_copy(d).wait_recv()
    ids = jnp.concatenate([all_ids[r] for r in range(n)], axis=0)
    here = ids - me * rows_here
    mine = (here >= 0) & (here < rows_here)
    order = dot(jnp.where(mine, 1.0, 0.0).astype(BF), before)
    keys = jnp.where(mine, order.astype(jnp.int32), -1)
    for r in range(n):
        key[r] = keys[r : r + 1, :]
        local[r] = jnp.where(mine, here, 0)[r : r + 1, :].astype(F32)

    def pick(r):
        hit = iota((row_cap, tok), 0) == key[r]
        return jnp.sum(jnp.where(hit, local[r], 0.0), axis=1, keepdims=True).astype(jnp.int32)

    @pl.loop(0, n // 2)
    def _(i):
        first = lax.rem(me + 1 + 2 * i, n)
        second = lax.rem(me + 2 + 2 * i, n)
        index = jnp.concatenate([pick(first), pick(second)], axis=0)
        onehot = jnp.where(iota((2 * row_cap, rows_here), 1) == index, 1.0, 0.0).astype(BF)
        got = dot(onehot, table[...]).astype(BF)
        packed[first] = got[:row_cap]
        packed[second] = got[row_cap:]
        row_copy(2 * i + 1).start()

        @pl.when(i < n // 2 - 1)
        def _():
            row_copy(2 * i + 2).start()

    arrived[me] = packed[me]

    ids_c = ids_col[...]
    h_iota = iota((tok, n), 1)
    base = h_iota * rows_here
    hot_h = jnp.where((ids_c >= base) & (ids_c < base + rows_here), 1.0, 0.0)
    after = (iota((tok, tok), 0) > iota((tok, tok), 1)).astype(BF)
    ahead = dot(after, hot_h.astype(BF)) + (h_iota * row_cap).astype(F32)
    place = jnp.sum(ahead * hot_h, axis=1, keepdims=True).astype(jnp.int32)
    find = jnp.where(iota((tok, n * row_cap), 1) == place, 1.0, 0.0).astype(BF)
    t_iota = iota((tok, 1), 0)
    length = tok // seqs
    valid = jnp.zeros((tok, 1), F32)
    for s in range(seqs):
        inside = (t_iota >= s * length) & (t_iota < s * length + lens[s])
        valid = jnp.where(inside, 1.0, valid)
    for d in range(1, n):
        row_copy(d).wait_recv()
    emb = dot(find, arrived[...].reshape(n * row_cap, width))
    emb = jnp.where(valid > 0.5, emb, 0.0)
    embedded[...] = emb.astype(BF)
    mean_square = jnp.mean(emb * emb, axis=1, keepdims=True)
    normed = (emb * lax.rsqrt(mean_square + EPSILON) * gain[...]).astype(BF)
    for p in range(n):
        send_rows[p] = dot(chosen[p], normed).astype(BF)
    for d in range(1, n):
        nrm_copy(d).start()
    own_rows = pltpu.make_async_copy(send_rows.at[me], rows_in.at[me], own.at[1])
    own_rows.start()

    def to_grp(b, peer, send, recv):
        return pltpu.make_async_remote_copy(
            src_ref=cot_all.at[b], dst_ref=cot_all.at[b], send_sem=send, recv_sem=recv,
            device_id={"grp": peer}, device_id_type=MESH,
        )

    def across(d):
        peer = lax.rem(chip + d, chips) * 2 + core
        return to_grp(grp, peer, grp_s.at[d], grp_r.at[d])

    def to_mate(d):
        source = lax.rem(chip - d + chips, chips) * 2 + core
        return to_grp(source, mate, grp_f.at[d], grp_r.at[chips + d])

    for d in range(1, n):
        cot_copy(d).wait_recv()
    own_cot.wait()
    for d in range(1, chips):
        across(d).start()
    to_mate(0).start()
    for d in range(1, chips):
        across(d).wait_recv()
        to_mate(d).start()
    for d in range(chips):
        to_mate(d).wait_recv()
        to_mate(d).wait_send()
    for d in range(1, chips):
        across(d).wait_send()
    for d in range(1, n):
        nrm_copy(d).wait_recv()
        for copy in (ids_copy, row_copy, cot_copy, nrm_copy):
            copy(d).wait_send()
    own_rows.wait()


def sigmoid_of(v):
    return 1.0 / (1.0 + jnp.exp(-v))


def forward_kernel(rows, w_gate, w_up, w_down, out):
    n, _, cap, width = rows.shape
    x = rows[...].reshape(n * cap, width)
    gate = dot(x, w_gate[0])
    up = dot(x, w_up[0])
    active = (gate * sigmoid_of(gate) * up).astype(BF)
    out[...] = dot(active, w_down[0], ((1,), (1,))).astype(BF).reshape(n, 1, cap, width)


def grad_kernel(_, rows, cot, w_gate, w_up, w_down, o_gate, o_up, o_down):
    g, n, _, cap, width = rows.shape
    x = rows[...].reshape(g * n * cap, width)
    c = cot[...].reshape(g * n * cap, width)
    gate = dot(x, w_gate[0])
    up = dot(x, w_up[0])
    d_active = dot(c, w_down[0])
    sigmoid = sigmoid_of(gate)
    silu = gate * sigmoid
    active = (silu * up).astype(BF)
    d_gate = (d_active * up * sigmoid * (1.0 + gate * (1.0 - sigmoid))).astype(BF)
    d_up = (d_active * silu).astype(BF)
    o_down[0] = dot(c, active, ((0,), (0,)))
    o_gate[0] = dot(x, d_gate, ((0,), (0,)))
    o_up[0] = dot(x, d_up, ((0,), (0,)))


def mix_kernel(experts, expert_ids, gates, embedded, returned, out):
    tok = embedded.shape[0]
    ids = expert_ids[...]
    e_iota = iota((tok, experts), 1)
    hots = [e_iota == ids[:, k : k + 1] for k in range(TOP)]
    hot = jnp.where(hots[0], 1.0, jnp.where(hots[1], 1.0, 0.0)).astype(BF)
    after = (iota((tok, tok), 0) > iota((tok, tok), 1)).astype(BF)
    earlier = dot(after, hot)
    total = embedded[...].astype(F32)
    mixed = jnp.zeros_like(total)
    for k in range(TOP):
        rank = jnp.sum(jnp.where(hots[k], earlier, 0.0), axis=1, keepdims=True).astype(jnp.int32)
        slot = ids[:, k : k + 1] * CAP + rank
        pick = jnp.where(iota((tok, experts * CAP), 1) == slot, 1.0, 0.0).astype(BF)
        mixed = mixed + gates[:, k : k + 1] * dot(pick, returned[...])
    out[...] = (total + mixed).astype(BF)


def on_device(
    item_ids, lengths, expert_ids, gate_weights, table, norm_gain, w_gate, w_up, w_down, d_out
):
    n = lax.axis_size("ex")
    groups = lax.axis_size("grp")
    seqs, length = item_ids.shape
    tok = seqs * length
    width = table.shape[1]
    exp_here = w_gate.shape[0]
    hidden = w_gate.shape[2]
    part = hidden // groups
    experts = exp_here * n
    row_cap = tok // 4
    block = exp_here * CAP
    vmem = pl.BlockSpec(memory_space=pltpu.VMEM)
    dma = pltpu.SemaphoreType.DMA
    rows_in, cot_all, embedded = pl.pallas_call(
        functools.partial(fetch_kernel, n, groups, seqs, experts, row_cap),
        out_shape=(
            jax.ShapeDtypeStruct((n, block, width), BF),
            jax.ShapeDtypeStruct((groups, n, block, width), BF),
            jax.ShapeDtypeStruct((tok, width), BF),
        ),
        in_specs=[vmem, vmem, pl.BlockSpec(memory_space=pltpu.SMEM)] + [vmem] * 5,
        out_specs=(pl.BlockSpec(memory_space=pl.ANY), pl.BlockSpec(memory_space=pl.ANY), vmem),
        scratch_shapes=[
            pltpu.VMEM((n, 1, tok), jnp.int32),
            pltpu.VMEM((n, 1, tok), jnp.int32),
            pltpu.VMEM((n, 1, tok), F32),
            pltpu.VMEM((n, row_cap, width), BF),
            pltpu.VMEM((n, row_cap, width), BF),
            pltpu.VMEM((n, block, tok), BF),
            pltpu.VMEM((n, block, width), BF),
            pltpu.VMEM((n, block, width), BF),
        ]
        + [dma((n,))] * 8
        + [dma((groups,)), dma((groups,)), dma((groups,)), dma((2,))],
        compiler_params=pltpu.CompilerParams(
            collective_id=0, has_side_effects=True, vmem_limit_bytes=VMEM_BYTES
        ),
    )(
        item_ids.reshape(1, tok),
        item_ids.reshape(tok, 1),
        lengths,
        expert_ids.T,
        gate_weights.T,
        table,
        norm_gain.reshape(1, width),
        d_out,
    )
    rows_all = lax.all_gather(rows_in, "grp", axis=0)
    local_params = pltpu.CompilerParams(vmem_limit_bytes=VMEM_BYTES)
    flops = 2 * n * block * width * hidden
    whole = lambda: pl.BlockSpec((1, width, hidden), lambda j: (j, 0, 0))
    expert_out = pl.pallas_call(
        forward_kernel,
        grid=(exp_here,),
        in_specs=[pl.BlockSpec((n, 1, CAP, width), lambda j: (0, j, 0, 0)), whole(), whole(), whole()],
        out_specs=pl.BlockSpec((n, 1, CAP, width), lambda j: (0, j, 0, 0)),
        out_shape=jax.ShapeDtypeStruct((n, exp_here, CAP, width), BF),
        compiler_params=local_params,
        cost_estimate=pl.CostEstimate(flops=3 * flops, bytes_accessed=2**24, transcendentals=0),
    )(rows_in.reshape(n, exp_here, CAP, width), w_gate, w_up, w_down)
    returned = lax.all_to_all(
        expert_out.reshape(n, block, width), "ex", split_axis=0, concat_axis=0, tiled=True
    )
    shape = (groups, n, exp_here, CAP, width)
    rows_spec = lambda: pl.BlockSpec((groups, n, 1, CAP, width), lambda j, q: (0, 0, j, 0, 0))
    weight_spec = lambda: pl.BlockSpec((1, width, part), lambda j, q: (j, 0, q[0]))
    grads = pl.pallas_call(
        grad_kernel,
        grid_spec=pltpu.PrefetchScalarGridSpec(
            num_scalar_prefetch=1,
            grid=(exp_here,),
            in_specs=[rows_spec(), rows_spec(), weight_spec(), weight_spec(), weight_spec()],
            out_specs=[pl.BlockSpec((1, width, part), lambda j, q: (j, 0, 0))] * 3,
        ),
        out_shape=[jax.ShapeDtypeStruct((exp_here, width, part), F32)] * 3,
        compiler_params=local_params,
        cost_estimate=pl.CostEstimate(flops=6 * flops, bytes_accessed=2**24, transcendentals=0),
    )(
        lax.axis_index("grp").reshape(1).astype(jnp.int32),
        rows_all.reshape(shape),
        cot_all.reshape(shape),
        w_gate,
        w_up,
        w_down,
    )
    output = pl.pallas_call(
        functools.partial(mix_kernel, experts),
        in_specs=[vmem] * 4,
        out_specs=vmem,
        out_shape=jax.ShapeDtypeStruct((tok, width), BF),
        compiler_params=local_params,
        cost_estimate=pl.CostEstimate(flops=flops, bytes_accessed=2**22, transcendentals=0),
    )(expert_ids, gate_weights, embedded, returned.reshape(experts * CAP, width))
    return (output, grads[0], grads[1], grads[2])


def solution(mesh):
    placed = (
        P(("grp", "ex"), None),
        P(("grp", "ex")),
        P(("grp", "ex"), None),
        P(("grp", "ex"), None),
        P("ex", None),
        P(),
        P("ex", None, None),
        P("ex", None, None),
        P("ex", None, None),
        P(("grp", "ex"), None),
    )
    return jax.shard_map(
        on_device,
        mesh=mesh,
        in_specs=placed,
        out_specs=(
            P(("grp", "ex"), None),
            P("ex", None, "grp"),
            P("ex", None, "grp"),
            P("ex", None, "grp"),
        ),
        check_vma=False,
    )
```

time: 339 us -> 199 us (0.59)
  Pallas kernels: 0 us -> 132 us
  waiting for transfers between devices: 159 us -> 35.9 us
  matrix products: 44.4 us -> 0 us
  local copies, waits for them, and re-layouts: 47.7 us -> 4.42 us
  other arithmetic: 28.6 us -> 0 us
  blocking collectives: 27.9 us -> 0 us
  starting transfers between devices: 15.9 us -> 12.3 us
    pallas_call x0 -> x4, Pallas kernels: none -> 132 us  [the longest x1 102 us: on_device(): pl.pallas_call(functools.partial(fetch_kernel, n, groups, seqs, experts,...]
    reduce_scatter x3 -> x0, waiting for transfers between devices: 62.1 us -> none  [the longest x1 44.3 us: on_device(): lax.psum_scatter(part_down.astype(jnp.bfloat16), 'grp', scatter_dimension...]
    all_to_all x4 -> x1, waiting for transfers between devices: 97.1 us -> 35.9 us  [on_device(): lax.all_to_all(expert_out.reshape(n, block, width), 'ex', split_axis=0, c...]
    dot_general x7 -> x0, matrix products: 44.4 us -> none  [the longest x1 10 us: on_device(): jnp.einsum('sjcd,jdf->sjcf', inbound_cot, w_down, preferred_element_type=...]
    scatter x3 -> x0, local copies, waits for them, and re-layouts: 28.7 us -> none  [the longest x1 15.5 us: on_device(): jnp.zeros((dump + 1,), jnp.int32).at[slot].set(local_rows)[:dump]]
    all_gather x1 -> x0, blocking collectives: 27.9 us -> none  [on_device(): every_id = lax.all_gather(item_ids, 'ex', axis=0, tiled=True).reshape(-1)]
    gather x4 -> x0, local copies, waits for them, and re-layouts: 13.1 us -> none  [the longest x1 6.72 us: on_device(): jnp.take(table, index_buffer, axis=0).reshape(ex_count, row_cap, width)]
    another operation x8 -> x0, other arithmetic: 11.6 us -> none
  transfers between devices with their start and end apart: 7 -> 2, of which waited for: 6 -> 1; matrix products, arithmetic and copies ran while one was open for 20% -> 1% of each run, Pallas kernels for 0% -> 7%
where the time goes in v1:
time: 199 us
  Pallas kernels  132 us (66%)
  waiting for transfers between devices  35.9 us (18%)
  between operations  14.1 us (7%)
  starting transfers between devices  12.3 us (6%)
  local copies, waits for them, and re-layouts  4.42 us (2%)
    pallas_call x1, Pallas kernels, on_device(): pl.pallas_call(functools.partial(fetch_kernel, n, groups, seqs, experts,...  102 us
    all_to_all x1, waiting for transfers between devices, on_device(): lax.all_to_all(expert_out.reshape(n, block, width), 'ex', split_axis=0, c...  35.9 us
    pallas_call x1, Pallas kernels, on_device(): pl.pallas_call(grad_kernel, grid_spec=pltpu.PrefetchScalarGridSpec(num_sc...  15.2 us
    all_to_all x1, starting transfers between devices, on_device(): lax.all_to_all(expert_out.reshape(n, block, width), 'ex', split_axis=0, c...  12.3 us
    pallas_call x1, Pallas kernels, on_device(): pl.pallas_call(forward_kernel, grid=(exp_here,), in_specs=[pl.BlockSpec((...  9.48 us
    pallas_call x1, Pallas kernels, on_device(): pl.pallas_call(functools.partial(mix_kernel, experts), in_specs=[vmem] *...  5.04 us
    unnamed x12, local copies, waits for them, and re-layouts  4.42 us
  transfers between devices with their start and end apart: 2, of which 1 were waited for; matrix products, arithmetic and copies ran while one was open for 1% of the time, Pallas kernels for 7%

profile of v1, /device:TPU:0, one launch (start us, length us, event | category | flops | bytes accessed | tf_op | source)
XLA Modules:
  0.0 198.9 jit_solution(7164120709246746551)
XLA Ops:
  7.2 0.0 all-gather.3.cloned.1.call-start
  7.2 0.7 copy.22
  7.9 0.0 copy-start.1
  7.9 0.9 copy.24
  8.8 0.0 copy-done.1
  8.8 102.5 %shard_map.129 = (bf16[8,192,512]{2,1,0:T(8,128)(2,1)}, bf16[4,8,192,512]{3,2,1,0:T(8,128)(2,1)}, bf16[512,512]{1,0:T(8,128)(2,1)}) custom-call(s32[1,512]{1,0:T(1,128)} %bitcast.21, s32[512,1]{1,0:T(8,128)} %bitcast.19, s32[2]{0:T(128)} %lens.1, s32[2,512]{1,0:T(2,128)} %bitcast.22, f32[2,512]{1,0:T(2,128)} %bitcast.23, bf16[4096,512]{1,0:T(8,128)(2,1)} %table.1, ...), custom_call_target="tpu_custom_call" | custom-call | tf_op jit(solution)/shard_map/pallas_call | solution.py:254
  111.2 0.0 all-gather.3.cloned.1.call-update
  111.2 0.0 copy-start.2
  111.3 0.0 copy-start.3
  111.3 9.5 %shard_map.130 = bf16[8,4,48,512]{3,2,1,0:T(8,128)(2,1)} custom-call(bf16[8,4,48,512]{3,2,1,0:T(8,128)(2,1)} %bitcast.16, bf16[4,512,1024]{2,1,0:T(8,128)(2,1)} %w_gate.3, bf16[4,512,1024]{2,1,0:T(8,128)(2,1)} %w_up.3, bf16[4,512,1024]{2,1,0:T(8,128)(2,1)} %w_down.3), custom_call_target="tpu_custom_call" | custom-call | flops 4831838208 | bytes 16777216 | tf_op jit(solution)/shard_map/pallas_call | solution.py:292
  120.8 12.3 %all-to-all-start = ((bf16[8,192,512]{2,1,0:T(8,128)(2,1)}), bf16[8,192,512]{2,1,0:T(8,128)(2,1)S(1)}, u32[]{:S(2)}, u32[]{:S(2)}) async-start(bf16[8,192,512]{2,1,0:T(8,128)(2,1)} %bitcast.18), calls=%async_computation | async-start | bytes 3145728 | tf_op jit(solution)/shard_map/all_to_all | solution.py:301
  133.1 0.0 copy-done.2
  133.1 0.9 copy.20.expert_ids
  133.9 0.0 copy-done.3
  133.9 0.9 copy.21.gates
  134.8 35.9 %all-to-all-done = bf16[8,192,512]{2,1,0:T(8,128)(2,1)S(1)} async-done(((bf16[8,192,512]{2,1,0:T(8,128)(2,1)}), bf16[8,192,512]{2,1,0:T(8,128)(2,1)S(1)}, u32[]{:S(2)}, u32[]{:S(2)}) %all-to-all-start) | async-done | bytes 1572896 | tf_op jit(solution)/shard_map/all_to_all | solution.py:301
  170.7 0.0 copy-start
  170.7 1.1 copy-done
  171.8 5.0 %shard_map.131 = bf16[512,512]{1,0:T(8,128)(2,1)} custom-call(s32[512,2]{1,0:T(8,128)} %copy.20.expert_ids, f32[512,2]{1,0:T(8,128)} %copy.21.gates, bf16[512,512]{1,0:T(8,128)(2,1)} %get-tuple-element.10.embedded, bf16[1536,512]{1,0:T(8,128)(2,1)} %bitcast.17), custom_call_target="tpu_custom_call" | custom-call | flops 1610612736 | bytes 4194304 | tf_op jit(solution)/shard_map/pallas_call | solution.py:326
  176.8 0.0 all-gather.3.cloned.1.call-done
  176.8 15.2 %shard_map.132 = (f32[4,512,256]{2,1,0:T(8,128)}, f32[4,512,256]{2,1,0:T(8,128)}, f32[4,512,256]{2,1,0:T(8,128)}) custom-call(s32[1]{0:T(128)} %bitcast.6._, bf16[4,8,4,48,512]{4,3,2,1,0:T(8,128)(2,1)} %bitcast.27, bf16[4,8,4,48,512]{4,3,2,1,0:T(8,128)(2,1)} %bitcast.26, bf16[4,512,1024]{2,1,0:T(8,128)(2,1)} %w_gate.3, bf16[4,512,1024]{2,1,0:T(8,128)(2,1)} %w_up.3, ...), custom_call_target="tpu_custom_call" | custom-call | flops 9663676416 | bytes 16777216 | tf_op jit(solution)/shard_map/pallas_call | solution.py:307
Async XLA Ops:
  7.2 169.7 %all-gather.3.cloned.1.call-start = ((), (), s32[]{:S(2)}) async-start(), calls=%async_computation.1 | async-start | bytes 7864320 | tf_op jit(solution)/shard_map/all_gather | solution.py:288
  7.9 0.9 copy-start.1
  111.2 21.8 %copy-start.2 = (s32[512,2]{0,1:T(2,128)S(1)}, s32[512,2]{0,1:T(2,128)}, u32[]{:S(2)}) copy-start(s32[512,2]{0,1:T(2,128)} %param.12) | copy-start | bytes 12292
  111.3 22.7 %copy-start.3 = (f32[512,2]{0,1:T(2,128)S(1)}, f32[512,2]{0,1:T(2,128)}, u32[]{:S(2)}) copy-start(f32[512,2]{0,1:T(2,128)} %param.13) | copy-start | bytes 12292
  120.8 49.9 %all-to-all-start = ((bf16[8,192,512]{2,1,0:T(8,128)(2,1)}), bf16[8,192,512]{2,1,0:T(8,128)(2,1)S(1)}, u32[]{:S(2)}, u32[]{:S(2)}) async-start(bf16[8,192,512]{2,1,0:T(8,128)(2,1)} %bitcast.18), calls=%async_computation | async-start | bytes 3145728 | tf_op jit(solution)/shard_map/all_to_all | solution.py:301
  170.7 1.1 copy-start
Sparse Core Ops, SparseCore 0:
  111.4 52.8 all-gather.2

commit v2 on v1

v2 whole, which is shorter than its diff:
```python
import functools

import jax
import jax.numpy as jnp
from jax import lax
from jax.experimental import pallas as pl
from jax.experimental.pallas import tpu as pltpu
from jax.sharding import PartitionSpec as P

TOP = 2
CAP = 48
EPSILON = 1e-06
VMEM_BYTES = 60 * 1024 * 1024
MESH = pl.DeviceIdType.MESH
BF = jnp.bfloat16
F32 = jnp.float32


def iota(shape, dim):
    return lax.broadcasted_iota(jnp.int32, shape, dim)


def dot(a, b, dims=((1,), (0,))):
    return lax.dot_general(a, b, (dims, ((), ())), preferred_element_type=F32)


def sigmoid_of(v):
    return 1.0 / (1.0 + jnp.exp(-v))


def layer_kernel(
    n, groups, seqs, experts, row_cap,
    ids_row, ids_col, lens, e_row, g_row, e_col, g_col, gain, d_out, table_h, gate_h, up_h, down_h,
    out, o_gate, o_up, o_down,
    all_ids, key, local, packed, arrived, chosen, send_cot, send_rows, rows_all, cot_all,
    expert_out, returned, table, w_gate, w_up, w_down, stage,
    ids_s, ids_r, row_s, row_r, cot_s, cot_r, nrm_s, nrm_r, ret_s, ret_r,
    cx_s, cx_r, cm_s, cm_r, rx_s, rx_r, rm_s, rm_r, load_s, stage_s,
):
    me = lax.axis_index("ex")
    grp = lax.axis_index("grp")
    chips = groups // 2
    chip, core = grp // 2, grp % 2
    mate = chip * 2 + 1 - core
    rows_here, width = table.shape
    tok = ids_row.shape[1]
    exp_here = experts // n
    block = exp_here * CAP
    part = o_gate.shape[2]
    loads = [
        pltpu.make_async_copy(src, dst, load_s.at[i])
        for i, (src, dst) in enumerate(
            [(table_h, table), (gate_h, w_gate), (up_h, w_up), (down_h, w_down)]
        )
    ]
    for load in loads:
        load.start()

    barrier = pltpu.get_barrier_semaphore()
    for d in range(1, n):
        pl.semaphore_signal(barrier, inc=1, device_id={"ex": lax.rem(me + d, n)}, device_id_type=MESH)
    for d in range(1, chips):
        peer = lax.rem(chip + d, chips) * 2 + core
        pl.semaphore_signal(barrier, inc=1, device_id={"grp": peer}, device_id_type=MESH)
    pl.semaphore_signal(barrier, inc=1, device_id={"grp": mate}, device_id_type=MESH)
    pl.semaphore_wait(barrier, n - 1 + chips)

    def to_ex(src, dst, send, recv, d):
        peer = lax.rem(me + d, n)
        return pltpu.make_async_remote_copy(
            src_ref=src(peer), dst_ref=dst, send_sem=send.at[d], recv_sem=recv.at[d],
            device_id={"ex": peer}, device_id_type=MESH,
        )

    def ids_copy(d):
        return to_ex(lambda p: all_ids.at[me], all_ids.at[me], ids_s, ids_r, d)

    def row_copy(d):
        return to_ex(lambda p: packed.at[p], arrived.at[me], row_s, row_r, d)

    def cot_copy(d):
        return to_ex(lambda p: send_cot.at[p], cot_all.at[grp, me], cot_s, cot_r, d)

    def nrm_copy(d, j):
        return to_ex(
            lambda p: send_rows.at[p, j], rows_all.at[grp, j, me], nrm_s.at[j], nrm_r.at[j], d
        )

    def ret_copy(d, j):
        return to_ex(lambda p: expert_out.at[j, p], returned.at[me, j], ret_s.at[j], ret_r.at[j], d)

    def across(held, send, recv, d):
        peer = lax.rem(chip + d, chips) * 2 + core
        return pltpu.make_async_remote_copy(
            src_ref=held(grp), dst_ref=held(grp), send_sem=send.at[d], recv_sem=recv.at[d],
            device_id={"grp": peer}, device_id_type=MESH,
        )

    def to_mate(held, send, recv, d):
        source = lax.rem(chip - d + chips, chips) * 2 + core
        return pltpu.make_async_remote_copy(
            src_ref=held(source), dst_ref=held(source), send_sem=send.at[d], recv_sem=recv.at[d],
            device_id={"grp": mate}, device_id_type=MESH,
        )

    def cot_across(d):
        return across(lambda b: cot_all.at[b], cx_s, cx_r, d)

    def cot_mate(d):
        return to_mate(lambda b: cot_all.at[b], cm_s, cm_r, d)

    def rows_across(d, j):
        return across(lambda b: rows_all.at[b, j], rx_s.at[j], rx_r.at[j], d)

    def rows_mate(d, j):
        return to_mate(lambda b: rows_all.at[b, j], rm_s.at[j], rm_r.at[j], d)

    all_ids[me] = ids_row[...]
    for d in range(1, n):
        ids_copy(d).start()

    before = (iota((tok, tok), 0) < iota((tok, tok), 1)).astype(BF)
    e0, e1 = e_row[0:1, :], e_row[1:2, :]
    e_iota = iota((experts, tok), 0)
    hot0, hot1 = e_iota == e0, e_iota == e1
    hot = jnp.where(hot0, 1.0, jnp.where(hot1, 1.0, 0.0)).astype(BF)
    earlier = dot(hot, before)
    slot0 = e0 * CAP + jnp.sum(jnp.where(hot0, earlier, 0.0), axis=0, keepdims=True).astype(jnp.int32)
    slot1 = e1 * CAP + jnp.sum(jnp.where(hot1, earlier, 0.0), axis=0, keepdims=True).astype(jnp.int32)
    g0, g1 = g_row[0:1, :], g_row[1:2, :]
    for p in range(n):
        s_iota = iota((block, tok), 0) + p * block
        m0, m1 = s_iota == slot0, s_iota == slot1
        weight = jnp.sum(jnp.where(m0, g0, jnp.where(m1, g1, 0.0)), axis=1, keepdims=True)
        chosen[p] = jnp.where(m0, 1.0, jnp.where(m1, 1.0, 0.0)).astype(BF)
        mine_cot = weight * dot(chosen[p], d_out[...])
        send_cot[p] = mine_cot.astype(BF).reshape(exp_here, CAP, width)
    for d in range(1, n):
        cot_copy(d).start()
    cot_all[grp, me] = send_cot[me]

    for d in range(1, n):
        ids_copy(d).wait_recv()
    ids = jnp.concatenate([all_ids[r] for r in range(n)], axis=0)
    here = ids - me * rows_here
    mine = (here >= 0) & (here < rows_here)
    order = dot(jnp.where(mine, 1.0, 0.0).astype(BF), before)
    keys = jnp.where(mine, order.astype(jnp.int32), -1)
    for r in range(n):
        key[r] = keys[r : r + 1, :]
        local[r] = jnp.where(mine, here, 0)[r : r + 1, :].astype(F32)

    def pick(r):
        hit = iota((row_cap, tok), 0) == key[r]
        return jnp.sum(jnp.where(hit, local[r], 0.0), axis=1, keepdims=True).astype(jnp.int32)

    loads[0].wait()

    @pl.loop(0, n // 2)
    def _(i):
        first = lax.rem(me + 1 + 2 * i, n)
        second = lax.rem(me + 2 + 2 * i, n)
        index = jnp.concatenate([pick(first), pick(second)], axis=0)
        onehot = jnp.where(iota((2 * row_cap, rows_here), 1) == index, 1.0, 0.0).astype(BF)
        got = dot(onehot, table[...]).astype(BF)
        packed[first] = got[:row_cap]
        packed[second] = got[row_cap:]
        row_copy(2 * i + 1).start()

        @pl.when(i < n // 2 - 1)
        def _():
            row_copy(2 * i + 2).start()

    arrived[me] = packed[me]

    ids_c = ids_col[...]
    h_iota = iota((tok, n), 1)
    base = h_iota * rows_here
    hot_h = jnp.where((ids_c >= base) & (ids_c < base + rows_here), 1.0, 0.0)
    after = (iota((tok, tok), 0) > iota((tok, tok), 1)).astype(BF)
    ahead = dot(after, hot_h.astype(BF)) + (h_iota * row_cap).astype(F32)
    place = jnp.sum(ahead * hot_h, axis=1, keepdims=True).astype(jnp.int32)
    find = jnp.where(iota((tok, n * row_cap), 1) == place, 1.0, 0.0).astype(BF)
    t_iota = iota((tok, 1), 0)
    length = tok // seqs
    valid = jnp.zeros((tok, 1), F32)
    for s in range(seqs):
        inside = (t_iota >= s * length) & (t_iota < s * length + lens[s])
        valid = jnp.where(inside, 1.0, valid)
    col = e_col[...]
    c_iota = iota((tok, experts), 1)
    hots = [c_iota == col[:, k : k + 1] for k in range(TOP)]
    spans = experts * CAP // width
    hot_c = jnp.where(hots[0], 1.0, jnp.where(hots[1], 1.0, 0.0)).astype(BF)
    earlier_c = dot(after, hot_c)
    for k in range(TOP):
        rank = jnp.sum(jnp.where(hots[k], earlier_c, 0.0), axis=1, keepdims=True)
        slot = col[:, k : k + 1] * CAP + rank.astype(jnp.int32)
        for i in range(spans):
            hit = iota((tok, width), 1) + i * width == slot
            table[pl.ds((k * spans + i) * tok, tok)] = jnp.where(hit, 1.0, 0.0).astype(BF)

    for d in range(1, n):
        cot_copy(d).wait_recv()
    for d in range(1, chips):
        cot_across(d).start()
    cot_mate(0).start()

    for d in range(1, n):
        row_copy(d).wait_recv()
    emb = dot(find, arrived[...].reshape(n * row_cap, width))
    emb = jnp.where(valid > 0.5, emb, 0.0)
    out[...] = emb.astype(BF)
    mean_square = jnp.mean(emb * emb, axis=1, keepdims=True)
    normed = (emb * lax.rsqrt(mean_square + EPSILON) * gain[...]).astype(BF)
    for p in range(n):
        send_rows[p] = dot(chosen[p], normed).astype(BF).reshape(exp_here, CAP, width)

    @pl.loop(0, exp_here)
    def _(j):
        for d in range(1, n):
            nrm_copy(d, j).start()
        rows_all[grp, j, me] = send_rows[me, j]

    for d in range(1, chips):
        cot_across(d).wait_recv()
        cot_mate(d).start()
    for load in loads[1:]:
        load.wait()

    @pl.loop(0, exp_here)
    def _(j):
        for d in range(1, n):
            nrm_copy(d, j).wait_recv()
        for d in range(1, chips):
            rows_across(d, j).start()
        rows_mate(0, j).start()
        x = rows_all[grp, j].reshape(n * CAP, width)
        gate = dot(x, w_gate[j])
        up = dot(x, w_up[j])
        active = (gate * sigmoid_of(gate) * up).astype(BF)
        result = dot(active, w_down[j], ((1,), (1,))).astype(BF)
        expert_out[j] = result.reshape(n, CAP, width)
        for d in range(1, n):
            ret_copy(d, j).start()
        returned[me, j] = expert_out[j, me]

    for d in range(chips):
        cot_mate(d).wait_recv()

    def pass_on(j):
        for d in range(1, chips):
            rows_across(d, j).wait_recv()
            rows_mate(d, j).start()

    def write(j, k):
        target = (o_gate, o_up, o_down)[k]
        return pltpu.make_async_copy(stage.at[j % 2, k], target.at[j], stage_s.at[j % 2, k])

    pass_on(0)
    columns = pl.ds(pl.multiple_of(grp * part, part), part)

    @pl.loop(0, exp_here)
    def _(j):
        @pl.when(j < exp_here - 1)
        def _():
            pass_on(j + 1)

        for d in range(chips):
            rows_mate(d, j).wait_recv()

        @pl.when(j >= 2)
        def _():
            for k in range(3):
                write(j - 2, k).wait()

        few = max(1, min(groups, 256 // (n * n)))
        for b in range(0, groups, few):
            some = pl.ds(b, min(few, groups - b))
            x = rows_all[some, j].reshape(-1, width)
            c = cot_all[some, :, j].reshape(-1, width)
            gate = dot(x, w_gate[j, :, columns])
            up = dot(x, w_up[j, :, columns])
            d_active = dot(c, w_down[j, :, columns])
            sigmoid = sigmoid_of(gate)
            silu = gate * sigmoid
            active = (silu * up).astype(BF)
            d_gate = (d_active * up * sigmoid * (1.0 + gate * (1.0 - sigmoid))).astype(BF)
            d_up = (d_active * silu).astype(BF)
            for k, (left, right) in enumerate([(x, d_gate), (x, d_up), (c, active)]):
                term = dot(left, right, ((0,), (0,)))
                stage[j % 2, k] = term if b == 0 else stage[j % 2, k] + term
        for k in range(3):
            write(j, k).start()

    @pl.loop(0, exp_here)
    def _(j):
        for d in range(1, n):
            ret_copy(d, j).wait_recv()

    back = returned[...].reshape(experts * CAP, width)
    mixed = jnp.zeros((tok, width), F32)
    for k in range(TOP):
        picked = jnp.zeros((tok, width), F32)
        for i in range(spans):
            pick_part = table[pl.ds((k * spans + i) * tok, tok)]
            picked = picked + dot(pick_part, back[i * width : (i + 1) * width])
        mixed = mixed + g_col[:, k : k + 1] * picked
    out[...] = (out[...].astype(F32) + mixed).astype(BF)

    for j in range(max(0, exp_here - 2), exp_here):
        for k in range(3):
            write(j, k).wait()
    for d in range(1, n):
        for copy in (ids_copy, row_copy, cot_copy):
            copy(d).wait_send()
    for d in range(1, chips):
        cot_across(d).wait_send()
    for d in range(chips):
        cot_mate(d).wait_send()

    @pl.loop(0, exp_here)
    def _(j):
        for d in range(1, n):
            nrm_copy(d, j).wait_send()
            ret_copy(d, j).wait_send()
        for d in range(1, chips):
            rows_across(d, j).wait_send()
        for d in range(chips):
            rows_mate(d, j).wait_send()


def on_device(
    item_ids, lengths, expert_ids, gate_weights, table, norm_gain, w_gate, w_up, w_down, d_out
):
    n = lax.axis_size("ex")
    groups = lax.axis_size("grp")
    seqs, length = item_ids.shape
    tok = seqs * length
    width = table.shape[1]
    exp_here, _, hidden = w_gate.shape
    part = hidden // groups
    experts = exp_here * n
    row_cap = tok // 4
    block = exp_here * CAP
    chips = groups // 2
    vmem = pl.BlockSpec(memory_space=pltpu.VMEM)
    hbm = pl.BlockSpec(memory_space=pl.ANY)
    dma = pltpu.SemaphoreType.DMA
    grad = jax.ShapeDtypeStruct((exp_here, width, part), F32)
    return pl.pallas_call(
        functools.partial(layer_kernel, n, groups, seqs, experts, row_cap),
        out_shape=(jax.ShapeDtypeStruct((tok, width), BF), grad, grad, grad),
        in_specs=[vmem, vmem, pl.BlockSpec(memory_space=pltpu.SMEM)] + [vmem] * 6 + [hbm] * 4,
        out_specs=(vmem, hbm, hbm, hbm),
        scratch_shapes=[
            pltpu.VMEM((n, 1, tok), jnp.int32),
            pltpu.VMEM((n, 1, tok), jnp.int32),
            pltpu.VMEM((n, 1, tok), F32),
            pltpu.VMEM((n, row_cap, width), BF),
            pltpu.VMEM((n, row_cap, width), BF),
            pltpu.VMEM((n, block, tok), BF),
            pltpu.VMEM((n, exp_here, CAP, width), BF),
            pltpu.VMEM((n, exp_here, CAP, width), BF),
            pltpu.VMEM((groups, exp_here, n, CAP, width), BF),
            pltpu.VMEM((groups, n, exp_here, CAP, width), BF),
            pltpu.VMEM((exp_here, n, CAP, width), BF),
            pltpu.VMEM((n, exp_here, CAP, width), BF),
            pltpu.VMEM(table.shape, BF),
            pltpu.VMEM(w_gate.shape, BF),
            pltpu.VMEM(w_up.shape, BF),
            pltpu.VMEM(w_down.shape, BF),
            pltpu.VMEM((2, 3, width, part), F32),
        ]
        + [dma((n,))] * 6
        + [dma((exp_here, n))] * 4
        + [dma((chips,))] * 4
        + [dma((exp_here, chips))] * 4
        + [dma((4,)), dma((2, 3))],
        compiler_params=pltpu.CompilerParams(
            collective_id=0, has_side_effects=True, vmem_limit_bytes=VMEM_BYTES
        ),
    )(
        item_ids.reshape(1, tok),
        item_ids.reshape(tok, 1),
        lengths,
        expert_ids.T,
        gate_weights.T,
        expert_ids,
        gate_weights,
        norm_gain.reshape(1, width),
        d_out,
        table,
        w_gate,
        w_up,
        w_down,
    )


def solution(mesh):
    placed = (
        P(("grp", "ex"), None),
        P(("grp", "ex")),
        P(("grp", "ex"), None),
        P(("grp", "ex"), None),
        P("ex", None),
        P(),
        P("ex", None, None),
        P("ex", None, None),
        P("ex", None, None),
        P(("grp", "ex"), None),
    )
    return jax.shard_map(
        on_device,
        mesh=mesh,
        in_specs=placed,
        out_specs=(
            P(("grp", "ex"), None),
            P("ex", None, "grp"),
            P("ex", None, "grp"),
            P("ex", None, "grp"),
        ),
        check_vma=False,
    )
```

time: 199 us -> 152 us (0.76)
  waiting for transfers between devices: 35.9 us -> 0 us
  between operations: 14.1 us -> 0.65 us
  starting transfers between devices: 12.3 us -> 0 us
  local copies, waits for them, and re-layouts: 4.42 us -> 13.4 us
  Pallas kernels: 132 us -> 137 us
    all_to_all x1 -> x0, waiting for transfers between devices: 35.9 us -> none  [on_device(): lax.all_to_all(expert_out.reshape(n, block, width), 'ex', split_axis=0, c...]
    all_to_all x1 -> x0, starting transfers between devices: 12.3 us -> none  [on_device(): lax.all_to_all(expert_out.reshape(n, block, width), 'ex', split_axis=0, c...]
    unnamed x12 -> x14, local copies, waits for them, and re-layouts: 4.42 us -> 13.4 us
    pallas_call x4 -> x1, Pallas kernels: 132 us -> 137 us  [on_device(): pl.pallas_call(functools.partial(layer_kernel, n, groups, seqs, experts,...]
  transfers between devices with their start and end apart: 2 -> 0, of which waited for: 1 -> 0; matrix products, arithmetic and copies ran while one was open for 1% -> 0% of each run, Pallas kernels for 7% -> 0%
where the time goes in v2:
time: 152 us; the launch traced here: 151 us
  Pallas kernels  137 us (90%)
  local copies, waits for them, and re-layouts  13.4 us (9%)
    pallas_call x1, Pallas kernels, on_device(): pl.pallas_call(functools.partial(layer_kernel, n, groups, seqs, experts,...  137 us
    unnamed x14, local copies, waits for them, and re-layouts  13.4 us

profile of v2, /device:TPU:0, one launch (start us, length us, event | category | flops | bytes accessed | tf_op | source)
XLA Modules:
  0.0 150.8 jit_solution(16857942892165878496)
XLA Ops:
  0.6 0.7 copy.19
  1.3 0.0 copy-start.2
  1.3 0.9 copy.21
  2.2 1.5 %copy.17.e_col = s32[512,2]{1,0:T(8,128)} copy(s32[512,2]{0,1:T(2,128)} %param.12) | data formatting | bytes 8192 | tf_op args[2]
  3.7 1.5 %copy.18.g_col = f32[512,2]{1,0:T(8,128)} copy(f32[512,2]{0,1:T(2,128)} %param.13) | data formatting | bytes 8192 | tf_op args[3]
  5.3 0.0 copy-done.2
  5.3 136.8 %shard_map.129 = (bf16[512,512]{1,0:T(8,128)(2,1)}, f32[4,512,256]{2,1,0:T(8,128)}, f32[4,512,256]{2,1,0:T(8,128)}, f32[4,512,256]{2,1,0:T(8,128)}) custom-call(s32[1,512]{1,0:T(1,128)} %bitcast.12, s32[512,1]{1,0:T(8,128)} %bitcast.10, s32[2]{0:T(128)} %lens.1, s32[2,512]{1,0:T(2,128)} %bitcast.13, f32[2,512]{1,0:T(2,128)} %bitcast.14, ...), custom_call_target="tpu_custom_call" | custom-call | tf_op jit(solution)/shard_map/pallas_call | solution.py:351
  142.0 1.9 %copy.26 = bf16[512,512]{1,0:T(8,128)(2,1)} copy(bf16[512,512]{1,0:T(8,128)(2,1)} %get-tuple-element.8) | data formatting | bytes 1048576
  143.9 0.0 copy-start.1
  143.9 3.2 %copy.27 = f32[4,512,256]{2,1,0:T(8,128)} copy(f32[4,512,256]{2,1,0:T(8,128)} %get-tuple-element.9) | data formatting | bytes 4194304
  147.1 0.0 copy-done.1
  147.1 0.0 copy-start
  147.1 1.3 copy.28
  148.4 1.0 copy-done
  149.4 1.3 copy.29
Async XLA Ops:
  1.3 3.9 %copy-start.2 = (s32[1,1,2,256]{3,1,2,0:T(1,128)}, s32[1,1,2,256]{3,1,2,0:T(1,128)S(1)}, u32[]{:S(2)}) copy-start(s32[1,1,2,256]{3,1,2,0:T(1,128)S(1)} %copy.19) | copy-start | bytes 6148
  143.9 3.2 %copy-start.1 = (f32[4,512,256]{2,1,0:T(8,128)S(1)}, f32[4,512,256]{2,1,0:T(8,128)}, u32[]{:S(2)}) copy-start(f32[4,512,256]{2,1,0:T(8,128)} %get-tuple-element.10) | copy-start | bytes 6291460
  147.1 2.3 %copy-start = (f32[4,512,256]{2,1,0:T(8,128)S(1)}, f32[4,512,256]{2,1,0:T(8,128)}, u32[]{:S(2)}) copy-start(f32[4,512,256]{2,1,0:T(8,128)} %get-tuple-element.11) | copy-start | bytes 6291460

commit v3 on v2

--- a/solution.py
+++ b/solution.py
@@ -30,7 +30,7 @@
 
 def layer_kernel(
     n, groups, seqs, experts, row_cap,
-    ids_row, ids_col, lens, e_row, g_row, e_col, g_col, gain, d_out, table_h, gate_h, up_h, down_h,
+    ids_here, lens, e_row, g_row, gain, d_out, table_h, gate_h, up_h, down_h,
     out, o_gate, o_up, o_down,
     all_ids, key, local, packed, arrived, chosen, send_cot, send_rows, rows_all, cot_all,
     expert_out, returned, table, w_gate, w_up, w_down, stage,
@@ -43,7 +43,7 @@
     chip, core = grp // 2, grp % 2
     mate = chip * 2 + 1 - core
     rows_here, width = table.shape
-    tok = ids_row.shape[1]
+    tok = e_row.shape[1]
     exp_here = experts // n
     block = exp_here * CAP
     part = o_gate.shape[2]
@@ -115,7 +115,8 @@
     def rows_mate(d, j):
         return to_mate(lambda b: rows_all.at[b, j], rm_s.at[j], rm_r.at[j], d)
 
-    all_ids[me] = ids_row[...]
+    ids_row = jnp.concatenate([ids_here[s : s + 1, :] for s in range(seqs)], axis=1)
+    all_ids[me] = ids_row
     for d in range(1, n):
         ids_copy(d).start()
 
@@ -128,6 +129,8 @@
     slot0 = e0 * CAP + jnp.sum(jnp.where(hot0, earlier, 0.0), axis=0, keepdims=True).astype(jnp.int32)
     slot1 = e1 * CAP + jnp.sum(jnp.where(hot1, earlier, 0.0), axis=0, keepdims=True).astype(jnp.int32)
     g0, g1 = g_row[0:1, :], g_row[1:2, :]
+    listed = [e0.astype(F32), e1.astype(F32), g0, g1, ids_row.astype(F32), jnp.zeros((3, tok), F32)]
+    columns_of = jnp.concatenate(listed, axis=0).T
     for p in range(n):
         s_iota = iota((block, tok), 0) + p * block
         m0, m1 = s_iota == slot0, s_iota == slot1
@@ -173,7 +176,7 @@
 
     arrived[me] = packed[me]
 
-    ids_c = ids_col[...]
+    ids_c = columns_of[:, 4:5].astype(jnp.int32)
     h_iota = iota((tok, n), 1)
     base = h_iota * rows_here
     hot_h = jnp.where((ids_c >= base) & (ids_c < base + rows_here), 1.0, 0.0)
@@ -187,7 +190,7 @@
     for s in range(seqs):
         inside = (t_iota >= s * length) & (t_iota < s * length + lens[s])
         valid = jnp.where(inside, 1.0, valid)
-    col = e_col[...]
+    col = columns_of[:, 0:2].astype(jnp.int32)
     c_iota = iota((tok, experts), 1)
     hots = [c_iota == col[:, k : k + 1] for k in range(TOP)]
     spans = experts * CAP // width
@@ -305,7 +308,7 @@
         for i in range(spans):
             pick_part = table[pl.ds((k * spans + i) * tok, tok)]
             picked = picked + dot(pick_part, back[i * width : (i + 1) * width])
-        mixed = mixed + g_col[:, k : k + 1] * picked
+        mixed = mixed + columns_of[:, 2 + k : 3 + k] * picked
     out[...] = (out[...].astype(F32) + mixed).astype(BF)
 
     for j in range(max(0, exp_here - 2), exp_here):
@@ -351,7 +354,7 @@
     return pl.pallas_call(
         functools.partial(layer_kernel, n, groups, seqs, experts, row_cap),
         out_shape=(jax.ShapeDtypeStruct((tok, width), BF), grad, grad, grad),
-        in_specs=[vmem, vmem, pl.BlockSpec(memory_space=pltpu.SMEM)] + [vmem] * 6 + [hbm] * 4,
+        in_specs=[vmem, pl.BlockSpec(memory_space=pltpu.SMEM)] + [vmem] * 4 + [hbm] * 4,
         out_specs=(vmem, hbm, hbm, hbm),
         scratch_shapes=[
             pltpu.VMEM((n, 1, tok), jnp.int32),
@@ -381,13 +384,10 @@
             collective_id=0, has_side_effects=True, vmem_limit_bytes=VMEM_BYTES
         ),
     )(
-        item_ids.reshape(1, tok),
-        item_ids.reshape(tok, 1),
+        item_ids,
         lengths,
         expert_ids.T,
         gate_weights.T,
-        expert_ids,
-        gate_weights,
         norm_gain.reshape(1, width),
         d_out,
         table,

time: 152 us -> 147 us (0.967)
  local copies, waits for them, and re-layouts: 13.4 us -> 8.73 us
    unnamed x14 -> x8, local copies, waits for them, and re-layouts: 13.4 us -> 8.73 us
where the time goes in v3:
time: 147 us; the launch traced here: 146 us
  Pallas kernels  137 us (93%)
  local copies, waits for them, and re-layouts  8.73 us (6%)
    pallas_call x1, Pallas kernels, on_device(): pl.pallas_call(functools.partial(layer_kernel, n, groups, seqs, experts,...  137 us
    unnamed x8, local copies, waits for them, and re-layouts  8.73 us

profile of v3, /device:TPU:0, one launch (start us, length us, event | category | flops | bytes accessed | tf_op | source)
XLA Modules:
  0.0 145.9 jit_solution(9023990069202182497)
XLA Ops:
  0.6 136.5 %shard_map.129 = (bf16[512,512]{1,0:T(8,128)(2,1)}, f32[4,512,256]{2,1,0:T(8,128)}, f32[4,512,256]{2,1,0:T(8,128)}, f32[4,512,256]{2,1,0:T(8,128)}) custom-call(s32[2,256]{1,0:T(2,128)} %ids_here.1, s32[2]{0:T(128)} %lens.1, s32[2,512]{1,0:T(2,128)} %bitcast.3, f32[2,512]{1,0:T(2,128)} %bitcast.4, f32[1,512]{1,0:T(1,128)} %bitcast.5, ...), custom_call_target="tpu_custom_call" | custom-call | tf_op jit(solution)/shard_map/pallas_call | solution.py:354
  137.2 1.9 %copy.18 = bf16[512,512]{1,0:T(8,128)(2,1)} copy(bf16[512,512]{1,0:T(8,128)(2,1)} %get-tuple-element.8) | data formatting | bytes 1048576
  139.0 0.0 copy-start.1
  139.0 3.2 %copy.19 = f32[4,512,256]{2,1,0:T(8,128)} copy(f32[4,512,256]{2,1,0:T(8,128)} %get-tuple-element.9) | data formatting | bytes 4194304
  142.2 0.0 copy-done.1
  142.2 0.0 copy-start
  142.2 1.3 copy.20
  143.6 1.0 copy-done
  144.6 1.3 copy.21
Async XLA Ops:
  139.0 3.2 %copy-start.1 = (f32[4,512,256]{2,1,0:T(8,128)S(1)}, f32[4,512,256]{2,1,0:T(8,128)}, u32[]{:S(2)}) copy-start(f32[4,512,256]{2,1,0:T(8,128)} %get-tuple-element.10) | copy-start | bytes 6291460
  142.2 2.3 %copy-start = (f32[4,512,256]{2,1,0:T(8,128)S(1)}, f32[4,512,256]{2,1,0:T(8,128)}, u32[]{:S(2)}) copy-start(f32[4,512,256]{2,1,0:T(8,128)} %get-tuple-element.11) | copy-start | bytes 6291460
